TPU v7x, 32 devices: a whole 2x2x4 slice. The times are simulated.
32 devices in a mesh: grp: 2 (over y), tp: 4 (over z), ap: 2 (over x), sq: 2 (over core).
Axes of the slice: x: 2, y: 2, z: 4, core: 2. Of those that a mesh axis runs over, the one named last changes fastest.
Arguments:
- heads_out: bfloat16 [4096, 8192], P(('grp', 'ap', 'sq'), 'tp'), parts along dimension 0, may hold values from -6 to 6
- base_weight: bfloat16 [8192, 8192], P('tp'), may hold values from -0.09375 to 0.09375
- shrink_store: bfloat16 [32, 64, 8192], P('ap', None, 'tp'), may hold values from -0.0625 to 0.0625
- expand_store: bfloat16 [32, 64, 8192], P('ap', None, 'tp'), may hold values from -0.75 to 0.75
- request_adapter: int32 [16], P(('grp', 'ap', 'sq')), parts along dimension 0, may hold values from 0 to 31
- adapter_slot: int32 [32], replicated, may hold values from 0 to 31, each once
- prompt_length: int32 [16], P(('grp', 'ap', 'sq')), parts along dimension 0, may hold values from 1 to 256, as said below
Outputs:
- projected: bfloat16 [4096, 8192], P(('grp', 'ap', 'sq'), 'tp'), parts along dimension 0
There are 2 independent parts, one for each index of `grp`. A program takes and returns all parts, laid end to end along the dimension named above; an argument that names none is the same for every part. Nothing has to cross between parts.
Inputs may be any that keep to these rules, and one draw needn't show every extreme that they name: `prompt_length`: among the 2 requests of each device one has the full length 256. `adapter_slot`: each slot appears once.
All inputs are finite; a program needn't handle non-finite values.
Results may differ from a plain program's by a relative error of at most 0.001.
Values may be sent and summed in bfloat16 or wider, within the bound.
A program may use at most 192 MiB of HBM per device.

v0:
```python
import jax
import jax.numpy as jnp
from jax import lax
from jax.sharding import PartitionSpec as P


def on_device(
    heads_out, base_weight, shrink_store, expand_store, request_adapter, adapter_slot, prompt_length
):
    req_count = request_adapter.shape[0]
    slot_rows = heads_out.shape[0] // req_count
    width_part = heads_out.shape[1]
    adapter_total = adapter_slot.shape[0]
    matches = request_adapter[:, None] == jnp.arange(adapter_total, dtype=jnp.int32)[None, :]
    slot_ids = jnp.sum(jnp.where(matches, adapter_slot[None, :], 0), axis=1)
    pieces = (
        lax.all_gather(shrink_store, "ap", axis=0, tiled=True),
        lax.all_gather(expand_store, "ap", axis=0, tiled=True),
    )
    piece_count = pieces[0].shape[0]
    onehot = (slot_ids[:, None] == jnp.arange(piece_count, dtype=jnp.int32)[None, :]).astype(
        jnp.bfloat16
    )
    down_part = jnp.einsum("qa,akd->qkd", onehot, pieces[0], preferred_element_type=jnp.float32)
    up_part = jnp.einsum("qa,akd->qkd", onehot, pieces[1], preferred_element_type=jnp.float32)
    down_sel = down_part
    up_sel = up_part
    down_sel = down_sel.astype(jnp.bfloat16)
    up_sel = up_sel.astype(jnp.bfloat16)
    blocks = heads_out.reshape(req_count, slot_rows, width_part)
    rank_part = jnp.einsum("qsd,qkd->qsk", blocks, down_sel, preferred_element_type=jnp.float32)
    rank_act = lax.psum(rank_part, "tp")
    expanded = jnp.einsum(
        "qsk,qkn->qsn", rank_act, up_sel.astype(jnp.float32), precision=lax.Precision.HIGHEST
    )
    base_part = jnp.dot(heads_out, base_weight, preferred_element_type=jnp.float32)
    base_share = lax.psum_scatter(base_part, "tp", scatter_dimension=1, tiled=True)
    total = base_share.reshape(req_count, slot_rows, -1) + expanded
    live = jnp.arange(slot_rows, dtype=jnp.int32)[None, :] < prompt_length[:, None]
    total = jnp.where(live[:, :, None], total, jnp.float32(0.0))
    return total.reshape(req_count * slot_rows, -1).astype(jnp.bfloat16)


def solution(mesh):
    return jax.shard_map(
        on_device,
        mesh=mesh,
        in_specs=(
            P(("grp", "ap", "sq"), "tp"),
            P("tp", None),
            P("ap", None, "tp"),
            P("ap", None, "tp"),
            P(("grp", "ap", "sq")),
            P(),
            P(("grp", "ap", "sq")),
        ),
        out_specs=P(("grp", "ap", "sq"), "tp"),
        check_vma=False,
    )
```

profile of v0, /device:TPU:0, one launch (start us, length us, event | category | flops | bytes accessed | tf_op | source)
XLA Modules:
  0.0 552.5 jit_solution(14200631440930452337)
XLA Ops:
  6.5 0.0 copy-start
  6.5 0.0 copy-start.2
  6.5 0.0 copy-start.3
  6.5 0.0 all-gather.3.cloned.1.call-start
  6.5 0.7 all-gather.3.cloned.1.call-update
  7.3 0.0 all-gather.5.cloned.1.call-start
  7.3 0.7 all-gather.5.cloned.1.call-update
  8.0 0.0 all-reduce.2.cloned.1.call-start
  8.1 0.0 copy-done.2
  8.1 0.0 copy-done.3
  8.1 0.2 fusion.14
  8.3 107.4 %all-gather.3.cloned.1.call-done = bf16[32,64,2048]{2,1,0:T(8,128)(2,1)} async-done(((bf16[16,64,2048]{2,1,0:T(8,128)(2,1)}), bf16[32,64,2048]{2,1,0:T(8,128)(2,1)}) %all-gather.3.cloned.1.call-update) | async-done | bytes 8388624 | tf_op jit(solution)/shard_map/all_gather | solution.py:17
  115.6 12.5 %fusion.4 = bf16[2,64,2048]{2,0,1:T(2,128)(2,1)S(1)} fusion(bf16[32,64,2048]{2,1,0:T(8,128)(2,1)} %all-gather.3.cloned.1.call-done, s32[2]{0:T(128)S(1)} %fusion.14), kind=kOutput, calls=%fused_computation.5 | convolution fusion | flops 17039424 | bytes 8912904 | tf_op jit(solution)/shard_map/qa,akd->qkd/dot_general | solution.py:24
  128.1 0.0 copy-done
  128.1 1.4 convolution_bitcast_fusion
  129.6 0.0 all-reduce.2.cloned.1.call-update
  129.6 0.2 reduce-scatter.2.cloned.1.call-start
  129.8 28.1 %fusion.17 = f32[512,8192]{1,0:T(8,128)} fusion(bf16[512,2048]{1,0:T(8,128)(2,1)S(1)} %copy-done, bf16[2048,8192]{1,0:T(8,128)(2,1)} %param.8), kind=kOutput, calls=%fused_computation.18 | convolution fusion | flops 17179869184 | bytes 52428800 | tf_op jit(solution)/shard_map/dot_general | solution.py:36
  157.9 0.0 copy-start.4
  157.9 0.0 reduce-scatter.2.cloned.1.call-update
  157.9 0.6 copy-done.4
  158.6 0.1 iota_compare_fusion
  158.6 62.6 %all-gather.5.cloned.1.call-done = bf16[32,64,2048]{2,1,0:T(8,128)(2,1)} async-done(((bf16[16,64,2048]{2,1,0:T(8,128)(2,1)}), bf16[32,64,2048]{2,1,0:T(8,128)(2,1)}) %all-gather.5.cloned.1.call-update) | async-done | bytes 8388624 | tf_op jit(solution)/shard_map/all_gather | solution.py:18
  221.2 0.0 copy-start.1
  221.2 12.6 %fusion.7 = bf16[2,64,2048]{2,0,1:T(2,128)(2,1)S(1)} fusion(bf16[32,64,2048]{2,1,0:T(8,128)(2,1)} %all-gather.5.cloned.1.call-done, s32[2]{0:T(128)S(1)} %fusion.14), kind=kOutput, calls=%fused_computation.6 | convolution fusion | flops 17039424 | bytes 8912904 | tf_op jit(solution)/shard_map/qa,akd->qkd/dot_general | solution.py:25
  233.9 24.2 %all-reduce.2.cloned.1.call-done = f32[2,256,64]{1,2,0:T(8,128)} async-done(((f32[2,256,64]{1,2,0:T(8,128)}), f32[2,256,64]{1,2,0:T(8,128)}) %all-reduce.2.cloned.1.call-update) | async-done | bytes 131088 | tf_op jit(solution)/shard_map/psum | solution.py:32
  258.0 282.3 %reduce-scatter.2.cloned.1.call-done = f32[512,2048]{1,0:T(8,128)} async-done(((f32[512,8192]{1,0:T(8,128)}), f32[512,2048]{1,0:T(8,128)}) %reduce-scatter.2.cloned.1.call-update) | async-done | bytes 4194320 | tf_op jit(solution)/shard_map/reduce_scatter | solution.py:37
  540.3 5.6 %select_convert_fusion = bf16[2,256,2048]{2,1,0:T(8,128)(2,1)} fusion(f32[2,256,2048]{2,1,0:T(8,128)} %bitcast.15, f32[2,256,64]{1,2,0:T(8,128)} %all-reduce.2.cloned.1.call-done, pred[2,256]{1,0:T(4,128)(4,1)S(1)} %iota_compare_fusion, bf16[2,64,2048]{2,0,1:T(2,128)(2,1)S(1)} %fusion.7), kind=kOutput, calls=%fused_computation.4 | convolution fusion | flops 808452096 | bytes 6947328 | tf_op jit(solution)/shard_map/qsk,qkn->qsn/dot_general | solution.py:33
  546.0 0.0 copy-done.1
Async XLA Ops:
  6.5 121.6 %copy-start = (bf16[512,2048]{1,0:T(8,128)(2,1)S(1)}, bf16[512,2048]{1,0:T(8,128)(2,1)}, u32[]{:S(2)}) copy-start(bf16[512,2048]{1,0:T(8,128)(2,1)} %param.7) | copy-start | bytes 6291460
  6.5 1.5 copy-start.2
  6.5 1.5 copy-start.3
  6.5 109.1 %all-gather.3.cloned.1.call-start = ((), (), s32[]{:S(2)}) async-start(), calls=%async_computation.2 | async-start | bytes 12582912 | tf_op jit(solution)/shard_map/all_gather | solution.py:17
  7.3 214.0 %all-gather.5.cloned.1.call-start = ((), (), s32[]{:S(2)}) async-start(), calls=%async_computation.4 | async-start | bytes 12582912 | tf_op jit(solution)/shard_map/all_gather | solution.py:18
  8.0 250.0 %all-reduce.2.cloned.1.call-start = ((), (), s32[]{:S(2)}) async-start(), calls=%async_computation.3 | async-start | bytes 262144 | tf_op jit(solution)/shard_map/psum | solution.py:32
  129.6 410.7 %reduce-scatter.2.cloned.1.call-start = ((), (), s32[]{:S(2)}) async-start(), calls=%async_computation.1 | async-start | bytes 20971520 | tf_op jit(solution)/shard_map/reduce_scatter | solution.py:37
  157.9 0.7 copy-start.4
  221.2 324.7 %copy-start.1 = (bf16[512,2048]{1,0:T(8,128)(2,1)S(1)}, bf16[512,2048]{1,0:T(8,128)(2,1)}, u32[]{:S(2)}) copy-start(bf16[512,2048]{1,0:T(8,128)(2,1)} %param.7) | copy-start | bytes 6291460
Sparse Core Ops, SparseCore 0:
  8.9 106.6 all-gather.2
  117.2 103.9 all-gather.4
  223.5 34.4 all-reduce.1
  260.4 279.9 reduce-scatter.1
where the time goes:
time: 553 us; the launch traced here: 552 us
  waiting for transfers between devices  478 us (86%)
  matrix products  60.3 us (11%)
  between operations  13.2 us (2%)
    reduce_scatter x1, waiting for transfers between devices, on_device(): lax.psum_scatter(base_part, 'tp', scatter_dimension=1, tiled=True)  282 us
    all_gather x1, waiting for transfers between devices, on_device(): lax.all_gather(shrink_store, 'ap', axis=0, tiled=True)  107 us
    all_gather x1, waiting for transfers between devices, on_device(): lax.all_gather(expand_store, 'ap', axis=0, tiled=True)  62.6 us
    dot_general x1, matrix products, on_device(): jnp.dot(heads_out, base_weight, preferred_element_type=jnp.float32)  28.1 us
    psum x1, waiting for transfers between devices, on_device(): rank_act = lax.psum(rank_part, 'tp')  24.2 us
    dot_general x1, matrix products, on_device(): jnp.einsum('qa,akd->qkd', onehot, pieces[1], preferred_element_type=jnp.f...  12.6 us
    dot_general x1, matrix products, on_device(): jnp.einsum('qa,akd->qkd', onehot, pieces[0], preferred_element_type=jnp.f...  12.5 us
  transfers between devices with their start and end apart: 4, of which 4 were waited for; matrix products, arithmetic and copies ran while one was open for 10% of the time, Pallas kernels for 0%

commit v1 on v0

v1 whole, which is shorter than its diff:
```python
import functools

import jax
import jax.numpy as jnp
from jax import lax
from jax.experimental import pallas as pl
from jax.experimental.pallas import tpu as pltpu
from jax.sharding import PartitionSpec as P

MESH = pl.DeviceIdType.MESH
SLOTS = 3
TOP = 32500.0
STEPS = 64.0


def decode(ref, rows):
    power = ref[rows : rows + 16, :][0:1, :].astype(jnp.float32)
    scale = jnp.exp2(power * (1.0 / STEPS)) * (1.0 / TOP)
    return ref[0:rows, :].astype(jnp.float32) * scale


def encode(ref, value, rows):
    top = jnp.maximum(jnp.max(jnp.abs(value), axis=0, keepdims=True), 1e-30)
    power = jnp.ceil(jnp.log2(top) * STEPS)
    factor = jnp.exp2(power * (-1.0 / STEPS)) * TOP
    ref[0:rows, :] = jnp.round(value * factor).astype(jnp.int32).astype(jnp.int16)
    ref[rows : rows + 16, :] = (
        jnp.broadcast_to(power, (16, power.shape[1])).astype(jnp.int32).astype(jnp.int16)
    )


def line_kernel(
    n, chunks, cw, x_ref, w_ref, o_ref, inbox, outbox, wbuf, own_w, acc, recv_sem, send_sem, w_sem, own_sem
):
    i = lax.axis_index("tp")
    rows, depth = x_ref.shape
    bw = chunks * cw
    items = chunks * (n - 1)
    count_right = chunks * (n - 1 - i)
    count_left = chunks * i

    def weight_copy(way, k):
        block = jnp.where(way == 0, n - 1 - k // chunks, k // chunks)
        start = pl.multiple_of(block * bw + (k % chunks) * cw, cw)
        return pltpu.make_async_copy(
            w_ref.at[:, pl.ds(start, cw)], wbuf.at[way, k % 2], w_sem.at[way, k % 2]
        )

    def own_copy(c):
        start = pl.multiple_of(i * bw + c * cw, cw)
        return pltpu.make_async_copy(
            w_ref.at[:, pl.ds(start, cw)], own_w.at[c % 2], own_sem.at[c % 2]
        )

    def item_copy(way, k):
        target = jnp.clip(i + 1 - 2 * way, 0, n - 1)
        return pltpu.make_async_remote_copy(
            src_ref=outbox.at[way, k % SLOTS],
            dst_ref=inbox.at[way, k],
            send_sem=send_sem.at[way, k % SLOTS],
            recv_sem=recv_sem.at[way, k],
            device_id={"tp": target},
            device_id_type=MESH,
        )

    def count_of(way):
        return jnp.where(way == 0, count_right, count_left)

    @pl.when(count_right > 0)
    def _():
        weight_copy(0, 0).start()

    @pl.when(count_left > 0)
    def _():
        weight_copy(1, 0).start()

    own_copy(0).start()

    barrier = pltpu.get_barrier_semaphore()

    @pl.when(i > 0)
    def _():
        pl.semaphore_signal(barrier, inc=1, device_id={"tp": i - 1}, device_id_type=MESH)

    @pl.when(i < n - 1)
    def _():
        pl.semaphore_signal(barrier, inc=1, device_id={"tp": i + 1}, device_id_type=MESH)

    pl.semaphore_wait(barrier, jnp.where(i > 0, 1, 0) + jnp.where(i < n - 1, 1, 0))

    late = jnp.where(i >= n // 2, 1, 0)

    def step(t, carry):
        k = t // 2
        way = (t + late) % 2
        count = count_of(way)

        @pl.when(k < count)
        def _():
            weight_copy(way, k).wait()

            @pl.when(k + 1 < count)
            def _():
                weight_copy(way, k + 1).start()

            acc[...] = jnp.dot(
                x_ref[...], wbuf[way, k % 2], preferred_element_type=jnp.float32
            )

            @pl.when(jnp.where(way == 0, i, n - 1 - i) > 0)
            def _():
                item_copy(way, k).wait_recv()
                acc[...] += decode(inbox.at[way, k], rows)

            @pl.when(k >= SLOTS)
            def _():
                item_copy(way, k).wait_send()

            encode(outbox.at[way, k % SLOTS], acc[...], rows)
            item_copy(way, k).start()

        return carry

    lax.fori_loop(0, 2 * items, step, 0)

    def finish(c, carry):
        own_copy(c).wait()

        @pl.when(c + 1 < chunks)
        def _():
            own_copy(c + 1).start()

        acc[...] = jnp.dot(x_ref[...], own_w[c % 2], preferred_element_type=jnp.float32)

        @pl.when(i > 0)
        def _():
            k = count_right + c
            item_copy(0, k).wait_recv()
            acc[...] += decode(inbox.at[0, k], rows)

        @pl.when(i < n - 1)
        def _():
            k = count_left + c
            item_copy(1, k).wait_recv()
            acc[...] += decode(inbox.at[1, k], rows)

        o_ref[:, pl.ds(pl.multiple_of(c * cw, cw), cw)] = acc[...]
        return carry

    lax.fori_loop(0, chunks, finish, 0)

    def drain(t, carry):
        way = t // SLOTS
        count = count_of(way)
        k = count - 1 - t % SLOTS

        @pl.when(k >= 0)
        def _():
            item_copy(way, k).wait_send()

        return carry

    lax.fori_loop(0, 2 * SLOTS, drain, 0)


def line_sum(n, heads_out, base_weight):
    rows, depth = heads_out.shape
    width = base_weight.shape[1]
    bw = width // n
    cw = min(256, bw)
    chunks = bw // cw
    items = chunks * (n - 1)
    return pl.pallas_call(
        functools.partial(line_kernel, n, chunks, cw),
        out_shape=jax.ShapeDtypeStruct((rows, bw), jnp.float32),
        in_specs=[
            pl.BlockSpec(memory_space=pltpu.VMEM),
            pl.BlockSpec(memory_space=pl.ANY),
        ],
        out_specs=pl.BlockSpec(memory_space=pltpu.VMEM),
        scratch_shapes=[
            pltpu.VMEM((2, items, rows + 16, cw), jnp.int16),
            pltpu.VMEM((2, SLOTS, rows + 16, cw), jnp.int16),
            pltpu.VMEM((2, 2, depth, cw), jnp.bfloat16),
            pltpu.VMEM((2, depth, cw), jnp.bfloat16),
            pltpu.VMEM((rows, cw), jnp.float32),
            pltpu.SemaphoreType.DMA((2, items)),
            pltpu.SemaphoreType.DMA((2, SLOTS)),
            pltpu.SemaphoreType.DMA((2, 2)),
            pltpu.SemaphoreType.DMA((2,)),
        ],
        compiler_params=pltpu.CompilerParams(
            collective_id=0, has_side_effects=True, vmem_limit_bytes=48 * 1024 * 1024
        ),
        cost_estimate=pl.CostEstimate(
            flops=2 * rows * depth * width,
            bytes_accessed=2 * depth * width,
            transcendentals=0,
        ),
    )(heads_out, base_weight)


def on_device(
    n, heads_out, base_weight, shrink_store, expand_store, request_adapter, adapter_slot, prompt_length
):
    req_count = request_adapter.shape[0]
    slot_rows = heads_out.shape[0] // req_count
    width_part = heads_out.shape[1]
    held = shrink_store.shape[0]

    slot_ids = adapter_slot[request_adapter]
    wanted = lax.all_gather(slot_ids, "ap") - lax.axis_index("ap") * held
    here = ((wanted >= 0) & (wanted < held))[:, :, None, None]
    place = jnp.clip(wanted, 0, held - 1)
    zero = jnp.zeros((), shrink_store.dtype)
    picked = jnp.stack(
        [jnp.where(here, store[place], zero) for store in (shrink_store, expand_store)], axis=1
    )
    moved = lax.all_to_all(picked, "ap", 0, 0)
    factors = jnp.sum(moved.astype(jnp.float32), axis=0).astype(jnp.bfloat16)
    down, up = factors[0], factors[1]

    blocks = heads_out.reshape(req_count, slot_rows, width_part)
    rank_part = jnp.einsum("qsd,qkd->qsk", blocks, down, preferred_element_type=jnp.float32)
    rank_act = lax.psum(rank_part, "tp")
    base_share = line_sum(n, heads_out, base_weight)
    expanded = jnp.einsum(
        "qsk,qkn->qsn", rank_act, up.astype(jnp.float32), precision=lax.Precision.HIGHEST
    )
    total = base_share.reshape(req_count, slot_rows, -1) + expanded
    live = jnp.arange(slot_rows, dtype=jnp.int32)[None, :] < prompt_length[:, None]
    total = jnp.where(live[:, :, None], total, jnp.float32(0.0))
    return total.reshape(req_count * slot_rows, -1).astype(jnp.bfloat16)


def solution(mesh):
    return jax.shard_map(
        functools.partial(on_device, mesh.shape["tp"]),
        mesh=mesh,
        in_specs=(
            P(("grp", "ap", "sq"), "tp"),
            P("tp", None),
            P("ap", None, "tp"),
            P("ap", None, "tp"),
            P(("grp", "ap", "sq")),
            P(),
            P(("grp", "ap", "sq")),
        ),
        out_specs=P(("grp", "ap", "sq"), "tp"),
        check_vma=False,
    )
```

time: 553 us -> 225 us (0.41)
  waiting for transfers between devices: 478 us -> 37.2 us
  Pallas kernels: 0 us -> 143 us
  matrix products: 60.3 us -> 7.03 us
  local copies, waits for them, and re-layouts: 0.65 us -> 7.94 us
    reduce_scatter x1 -> x0, waiting for transfers between devices: 282 us -> none  [on_device(): lax.psum_scatter(base_part, 'tp', scatter_dimension=1, tiled=True)]
    all_gather x2 -> x0, waiting for transfers between devices: 170 us -> none  [the longest x1 107 us: on_device(): lax.all_gather(shrink_store, 'ap', axis=0, tiled=True)]
    pallas_call x0 -> x1, Pallas kernels: none -> 143 us  [line_sum(): pl.pallas_call(functools.partial(line_kernel, n, chunks, cw), out_shape=j...]
    dot_general x5 -> x2, matrix products: 60.3 us -> 7.03 us  [the longest x1 5.61 us: on_device(): jnp.einsum('qsk,qkn->qsn', rank_act, up.astype(jnp.float32), precision=la...]
    psum x1, waiting for transfers between devices: 24.2 us -> 37.1 us  [on_device(): rank_act = lax.psum(rank_part, 'tp')]
    gather x0 -> x3, local copies, waits for them, and re-layouts: none -> 6.24 us  [the longest x2 5.6 us: on_device(): store[place]]
  transfers between devices with their start and end apart: 4 -> 2, of which waited for: 4 -> 1; matrix products, arithmetic and copies ran while one was open for 10% -> 0% of each run, Pallas kernels for 0% -> 64%
where the time goes in v1:
time: 225 us; the launch traced here: 224 us
  Pallas kernels  143 us (64%)
  waiting for transfers between devices  37.2 us (17%)
  between operations  14.2 us (6%)
  local copies, waits for them, and re-layouts  7.94 us (4%)
  matrix products  7.03 us (3%)
  blocking collectives  5.19 us (2%)
  starting transfers between devices  4.84 us (2%)
  other arithmetic  4.62 us (2%)
    pallas_call x1, Pallas kernels, line_sum(): pl.pallas_call(functools.partial(line_kernel, n, chunks, cw), out_shape=j...  143 us
    psum x1, waiting for transfers between devices, on_device(): rank_act = lax.psum(rank_part, 'tp')  37.1 us
    dot_general x1, matrix products, on_device(): jnp.einsum('qsk,qkn->qsn', rank_act, up.astype(jnp.float32), precision=la...  5.61 us
    gather x2, local copies, waits for them, and re-layouts, on_device(): store[place]  5.6 us
    unnamed x1, blocking collectives  5.19 us
    all_to_all x1, starting transfers between devices, on_device(): moved = lax.all_to_all(picked, 'ap', 0, 0)  4.8 us
  transfers between devices with their start and end apart: 2, of which 1 were waited for; matrix products, arithmetic and copies ran while one was open for 0% of the time, Pallas kernels for 64%

profile of v1, /device:TPU:0, one launch (start us, length us, event | category | flops | bytes accessed | tf_op | source)
XLA Modules:
  0.0 224.2 jit_solution(13354341875688701798)
XLA Ops:
  6.5 0.0 copy-start
  6.5 0.7 compare_select_fusion.1
  7.2 1.2 dynamic-slice
  9.1 0.0 copy-done
  9.1 0.6 gather_fusion
  9.8 0.2 dynamic-update-slice
  10.0 5.2 %all-reduce = s32[4]{0:T(128)S(1)} all-reduce(s32[4]{0:T(128)S(1)} %dynamic-update-slice), channel_id=2, replica_groups=mesh['grp'=2,'tp'=4,'ap'=2,'sq'=2] {'ap'}, use_global_device_ids=true, to_apply=%add | all-reduce | flops 4 | bytes 32
  15.2 0.1 reshape.87
  15.2 0.1 reshape.86
  15.3 0.1 reshape.56
  15.4 2.8 %gather_fusion.2 = bf16[4,64,2048]{2,1,0:T(8,128)(2,1)S(1)} fusion(bf16[16,64,2048]{2,1,0:T(8,128)(2,1)} %param.10, s32[1024]{0:T(1024)S(1)} %pad_clamp_fusion), kind=kCustom, calls=%fused_computation.2 | custom fusion | bytes 2097168 | tf_op jit(solution)/shard_map/gather | solution.py:217
  18.2 2.8 %gather_fusion.1 = bf16[4,64,2048]{2,1,0:T(8,128)(2,1)S(1)} fusion(bf16[16,64,2048]{2,1,0:T(8,128)(2,1)} %param.9, s32[1024]{0:T(1024)S(1)} %pad_clamp_fusion), kind=kCustom, calls=%fused_computation.1 | custom fusion | bytes 2097168 | tf_op jit(solution)/shard_map/gather | solution.py:217
  21.0 0.2 broadcast_select_fusion.1
  21.3 0.0 copy-start.1
  21.3 1.5 pad_maximum_fusion
  22.8 4.8 %all-to-all-start = ((bf16[2,2,2,64,2048]{4,3,2,1,0:T(8,128)(2,1)}), bf16[2,2,2,64,2048]{4,3,2,1,0:T(8,128)(2,1)}, u32[]{:S(2)}, u32[]{:S(2)}) async-start(bf16[2,2,2,64,2048]{4,3,2,1,0:T(8,128)(2,1)} %pad_maximum_fusion), calls=%async_computation | async-start | bytes 4194304 | tf_op jit(solution)/shard_map/all_to_all | solution.py:219
  27.6 0.0 all-reduce.3.cloned.1.call-start
  27.6 0.0 copy-done.1
  27.6 143.3 %shard_map.73 = f32[512,2048]{1,0:T(8,128)} custom-call(bf16[512,2048]{1,0:T(8,128)(2,1)S(1)} %copy-done.1, bf16[2048,8192]{1,0:T(8,128)(2,1)} %w_ref.1), custom_call_target="tpu_custom_call" | custom-call | flops 17179869184 | bytes 33554432 | tf_op jit(solution)/shard_map/pallas_call | solution.py:173
  170.9 0.0 copy-start.2
  170.9 0.0 all-to-all-done
  170.9 2.1 reduce_sum.12
  173.1 1.4 convolution_bitcast_fusion
  174.5 0.0 all-reduce.3.cloned.1.call-update
  174.5 0.0 copy-done.2
  174.5 0.1 iota_compare_fusion
  174.6 37.1 %all-reduce.3.cloned.1.call-done = f32[2,256,64]{1,2,0:T(8,128)} async-done(((f32[2,256,64]{1,2,0:T(8,128)}), f32[2,256,64]{1,2,0:T(8,128)}) %all-reduce.3.cloned.1.call-update) | async-done | bytes 131088 | tf_op jit(solution)/shard_map/psum | solution.py:225
  211.8 5.6 %select_convert_fusion = bf16[2,256,2048]{2,1,0:T(8,128)(2,1)} fusion(f32[2,256,2048]{2,1,0:T(8,128)} %bitcast.19, f32[2,256,64]{1,2,0:T(8,128)} %all-reduce.3.cloned.1.call-done, pred[2,256]{1,0:T(4,128)(4,1)S(1)} %iota_compare_fusion, bf16[2,2,64,2048]{3,2,1,0:T(8,128)(2,1)S(1)} %reduce_sum.12), kind=kOutput, calls=%fused_computation.3 | convolution fusion | flops 808452096 | bytes 6947840 | tf_op jit(solution)/shard_map/qsk,qkn->qsn/dot_general | solution.py:227
  (6 shorter events, 0.0 us)
Async XLA Ops:
  6.5 2.6 %copy-start = (s32[32]{0:T(128)S(1)}, s32[32]{0:T(128)}, u32[]{:S(2)}) copy-start(s32[32]{0:T(128)} %param.12) | copy-start | bytes 388
  21.3 6.4 %copy-start.1 = (bf16[512,2048]{1,0:T(8,128)(2,1)S(1)}, bf16[512,2048]{1,0:T(8,128)(2,1)}, u32[]{:S(2)}) copy-start(bf16[512,2048]{1,0:T(8,128)(2,1)} %x_ref.1) | copy-start | bytes 6291460
  22.8 148.2 %all-to-all-start = ((bf16[2,2,2,64,2048]{4,3,2,1,0:T(8,128)(2,1)}), bf16[2,2,2,64,2048]{4,3,2,1,0:T(8,128)(2,1)}, u32[]{:S(2)}, u32[]{:S(2)}) async-start(bf16[2,2,2,64,2048]{4,3,2,1,0:T(8,128)(2,1)} %pad_maximum_fusion), calls=%async_computation | async-start | bytes 4194304 | tf_op jit(solution)/shard_map/all_to_all | solution.py:219
  27.6 184.2 %all-reduce.3.cloned.1.call-start = ((), (), s32[]{:S(2)}) async-start(), calls=%async_computation.1 | async-start | bytes 262144 | tf_op jit(solution)/shard_map/psum | solution.py:225
  170.9 3.6 %copy-start.2 = (s32[2]{0:T(128)S(1)}, s32[2]{0:T(128)}, u32[]{:S(2)}) copy-start(s32[2]{0:T(128)} %param.13) | copy-start | bytes 28
Sparse Core Ops, SparseCore 0:
  174.6 37.0 all-reduce.2

commit v2 on v1

--- a/solution.py
+++ b/solution.py
@@ -30,14 +30,42 @@
 
 
 def line_kernel(
-    n, chunks, cw, x_ref, w_ref, o_ref, inbox, outbox, wbuf, own_w, acc, recv_sem, send_sem, w_sem, own_sem
+    n, n_ap, chunks, cw, req, x_ref, w_ref, picked_ref, length_ref, o_ref, inbox, outbox, wbuf, own_w, acc,
+    factors, up, rank_own, rank_in, rank_out, parts, recv_sem, send_sem, w_sem, own_sem,
+    factor_recv, factor_send, rank_recv, rank_send, local_sem,
 ):
     i = lax.axis_index("tp")
+    me = lax.axis_index("ap")
     rows, depth = x_ref.shape
+    slot_rows, lanes = rank_own.shape
+    rank = lanes // req
     bw = chunks * cw
     items = chunks * (n - 1)
+    middle = items // 3
     count_right = chunks * (n - 1 - i)
     count_left = chunks * i
+
+    def factor_copy(hop):
+        return pltpu.make_async_remote_copy(
+            src_ref=picked_ref.at[(me + hop) % n_ap],
+            dst_ref=factors.at[me],
+            send_sem=factor_send.at[hop],
+            recv_sem=factor_recv.at[hop],
+            device_id={"ap": (me + hop) % n_ap},
+            device_id_type=MESH,
+        )
+
+    def rank_copy(way):
+        return pltpu.make_async_remote_copy(
+            src_ref=rank_out.at[way],
+            dst_ref=rank_in.at[way],
+            send_sem=rank_send.at[way],
+            recv_sem=rank_recv.at[way],
+            device_id={"tp": jnp.clip(i + 1 - 2 * way, 0, n - 1)},
+            device_id_type=MESH,
+        )
+
+    own_factors = pltpu.make_async_copy(picked_ref.at[me], factors.at[me], local_sem)
 
     def weight_copy(way, k):
         block = jnp.where(way == 0, n - 1 - k // chunks, k // chunks)
@@ -75,6 +103,7 @@
         weight_copy(1, 0).start()
 
     own_copy(0).start()
+    own_factors.start()
 
     barrier = pltpu.get_barrier_semaphore()
 
@@ -86,7 +115,17 @@
     def _():
         pl.semaphore_signal(barrier, inc=1, device_id={"tp": i + 1}, device_id_type=MESH)
 
-    pl.semaphore_wait(barrier, jnp.where(i > 0, 1, 0) + jnp.where(i < n - 1, 1, 0))
+    for hop in range(1, n_ap):
+        pl.semaphore_signal(
+            barrier, inc=1, device_id={"ap": (me + hop) % n_ap}, device_id_type=MESH
+        )
+
+    pl.semaphore_wait(
+        barrier, n_ap - 1 + jnp.where(i > 0, 1, 0) + jnp.where(i < n - 1, 1, 0)
+    )
+
+    for hop in range(1, n_ap):
+        factor_copy(hop).start()
 
     late = jnp.where(i >= n // 2, 1, 0)
 
@@ -95,6 +134,37 @@
         way = (t + late) % 2
         count = count_of(way)
 
+        @pl.when(t == 2 * middle)
+        def _():
+            own_factors.wait()
+            for hop in range(1, n_ap):
+                factor_copy(hop).wait_recv()
+            down = factors[0, 0]
+            grow = factors[0, 1]
+            for source in range(1, n_ap):
+                down = down + factors[source, 0]
+                grow = grow + factors[source, 1]
+            up[...] = grow
+            full = lax.dot_general(
+                x_ref[...], down, (((1,), (1,)), ((), ())), preferred_element_type=jnp.float32
+            )
+            lane = lax.broadcasted_iota(jnp.int32, (slot_rows, lanes), 1)
+            total = full[0:slot_rows]
+            for q in range(1, req):
+                total = jnp.where(lane >= q * rank, full[q * slot_rows : (q + 1) * slot_rows], total)
+            rank_own[...] = total
+
+        @pl.when((k == middle) & (count > 0))
+        def _():
+            rank_out[way] = rank_own[...]
+
+            @pl.when(jnp.where(way == 0, i, n - 1 - i) > 0)
+            def _():
+                rank_copy(way).wait_recv()
+                rank_out[way] = rank_own[...] + rank_in[way]
+
+            rank_copy(way).start()
+
         @pl.when(k < count)
         def _():
             weight_copy(way, k).wait()
@@ -123,6 +193,32 @@
 
     lax.fori_loop(0, 2 * items, step, 0)
 
+    @pl.when(i == n - 1)
+    def _():
+        rank_copy(0).wait_recv()
+
+    @pl.when(i == 0)
+    def _():
+        rank_copy(1).wait_recv()
+
+    @pl.when(i > 0)
+    def _():
+        rank_own[...] += rank_in[0]
+
+    @pl.when(i < n - 1)
+    def _():
+        rank_own[...] += rank_in[1]
+
+    lane = lax.broadcasted_iota(jnp.int32, (slot_rows, lanes), 1)
+    for q in range(req):
+        left = jnp.where((lane >= q * rank) & (lane < (q + 1) * rank), rank_own[...], 0.0)
+        for term in range(3):
+            piece = left.astype(jnp.bfloat16)
+            parts[term, q * slot_rows : (q + 1) * slot_rows, :] = piece
+            left = left - piece.astype(jnp.float32)
+
+    position = lax.broadcasted_iota(jnp.int32, (slot_rows, cw), 0)
+
     def finish(c, carry):
         own_copy(c).wait()
 
@@ -130,7 +226,13 @@
         def _():
             own_copy(c + 1).start()
 
-        acc[...] = jnp.dot(x_ref[...], own_w[c % 2], preferred_element_type=jnp.float32)
+        here = pl.ds(pl.multiple_of(c * cw, cw), cw)
+        expanded = jnp.zeros((rows, cw), jnp.float32)
+        for term in (2, 1, 0):
+            expanded += jnp.dot(parts[term], up[:, here], preferred_element_type=jnp.float32)
+        acc[...] = expanded + jnp.dot(
+            x_ref[...], own_w[c % 2], preferred_element_type=jnp.float32
+        )
 
         @pl.when(i > 0)
         def _():
@@ -144,7 +246,11 @@
             item_copy(1, k).wait_recv()
             acc[...] += decode(inbox.at[1, k], rows)
 
-        o_ref[:, pl.ds(pl.multiple_of(c * cw, cw), cw)] = acc[...]
+        for q in range(req):
+            span = slice(q * slot_rows, (q + 1) * slot_rows)
+            o_ref[span, here] = jnp.where(
+                position < length_ref[q], acc[span, :], 0.0
+            ).astype(jnp.bfloat16)
         return carry
 
     lax.fori_loop(0, chunks, finish, 0)
@@ -162,20 +268,33 @@
 
     lax.fori_loop(0, 2 * SLOTS, drain, 0)
 
-
-def line_sum(n, heads_out, base_weight):
+    for hop in range(1, n_ap):
+        factor_copy(hop).wait_send()
+    for way in range(2):
+
+        @pl.when(count_of(way) > 0)
+        def _():
+            rank_copy(way).wait_send()
+
+
+def line_sum(n, n_ap, heads_out, base_weight, picked, prompt_length):
     rows, depth = heads_out.shape
     width = base_weight.shape[1]
+    req = prompt_length.shape[0]
+    lanes = picked.shape[2]
     bw = width // n
     cw = min(256, bw)
     chunks = bw // cw
     items = chunks * (n - 1)
+    slot_rows = rows // req
     return pl.pallas_call(
-        functools.partial(line_kernel, n, chunks, cw),
-        out_shape=jax.ShapeDtypeStruct((rows, bw), jnp.float32),
+        functools.partial(line_kernel, n, n_ap, chunks, cw, req),
+        out_shape=jax.ShapeDtypeStruct((rows, bw), jnp.bfloat16),
         in_specs=[
             pl.BlockSpec(memory_space=pltpu.VMEM),
             pl.BlockSpec(memory_space=pl.ANY),
+            pl.BlockSpec(memory_space=pl.ANY),
+            pl.BlockSpec(memory_space=pltpu.SMEM),
         ],
         out_specs=pl.BlockSpec(memory_space=pltpu.VMEM),
         scratch_shapes=[
@@ -184,10 +303,21 @@
             pltpu.VMEM((2, 2, depth, cw), jnp.bfloat16),
             pltpu.VMEM((2, depth, cw), jnp.bfloat16),
             pltpu.VMEM((rows, cw), jnp.float32),
+            pltpu.VMEM(picked.shape, jnp.bfloat16),
+            pltpu.VMEM((lanes, depth), jnp.bfloat16),
+            pltpu.VMEM((slot_rows, lanes), jnp.float32),
+            pltpu.VMEM((2, slot_rows, lanes), jnp.float32),
+            pltpu.VMEM((2, slot_rows, lanes), jnp.float32),
+            pltpu.VMEM((3, rows, lanes), jnp.bfloat16),
             pltpu.SemaphoreType.DMA((2, items)),
             pltpu.SemaphoreType.DMA((2, SLOTS)),
             pltpu.SemaphoreType.DMA((2, 2)),
             pltpu.SemaphoreType.DMA((2,)),
+            pltpu.SemaphoreType.DMA((n_ap,)),
+            pltpu.SemaphoreType.DMA((n_ap,)),
+            pltpu.SemaphoreType.DMA((2,)),
+            pltpu.SemaphoreType.DMA((2,)),
+            pltpu.SemaphoreType.DMA,
         ],
         compiler_params=pltpu.CompilerParams(
             collective_id=0, has_side_effects=True, vmem_limit_bytes=48 * 1024 * 1024
@@ -197,17 +327,14 @@
             bytes_accessed=2 * depth * width,
             transcendentals=0,
         ),
-    )(heads_out, base_weight)
+    )(heads_out, base_weight, picked, prompt_length)
 
 
 def on_device(
-    n, heads_out, base_weight, shrink_store, expand_store, request_adapter, adapter_slot, prompt_length
+    n, n_ap, heads_out, base_weight, shrink_store, expand_store, request_adapter, adapter_slot, prompt_length
 ):
-    req_count = request_adapter.shape[0]
-    slot_rows = heads_out.shape[0] // req_count
-    width_part = heads_out.shape[1]
-    held = shrink_store.shape[0]
-
+    held, rank, part = shrink_store.shape
+    req = request_adapter.shape[0]
     slot_ids = adapter_slot[request_adapter]
     wanted = lax.all_gather(slot_ids, "ap") - lax.axis_index("ap") * held
     here = ((wanted >= 0) & (wanted < held))[:, :, None, None]
@@ -216,26 +343,13 @@
     picked = jnp.stack(
         [jnp.where(here, store[place], zero) for store in (shrink_store, expand_store)], axis=1
     )
-    moved = lax.all_to_all(picked, "ap", 0, 0)
-    factors = jnp.sum(moved.astype(jnp.float32), axis=0).astype(jnp.bfloat16)
-    down, up = factors[0], factors[1]
-
-    blocks = heads_out.reshape(req_count, slot_rows, width_part)
-    rank_part = jnp.einsum("qsd,qkd->qsk", blocks, down, preferred_element_type=jnp.float32)
-    rank_act = lax.psum(rank_part, "tp")
-    base_share = line_sum(n, heads_out, base_weight)
-    expanded = jnp.einsum(
-        "qsk,qkn->qsn", rank_act, up.astype(jnp.float32), precision=lax.Precision.HIGHEST
-    )
-    total = base_share.reshape(req_count, slot_rows, -1) + expanded
-    live = jnp.arange(slot_rows, dtype=jnp.int32)[None, :] < prompt_length[:, None]
-    total = jnp.where(live[:, :, None], total, jnp.float32(0.0))
-    return total.reshape(req_count * slot_rows, -1).astype(jnp.bfloat16)
+    picked = picked.reshape(n_ap, 2, req * rank, part)
+    return line_sum(n, n_ap, heads_out, base_weight, picked, prompt_length)
 
 
 def solution(mesh):
     return jax.shard_map(
-        functools.partial(on_device, mesh.shape["tp"]),
+        functools.partial(on_device, mesh.shape["tp"], mesh.shape["ap"]),
         mesh=mesh,
         in_specs=(
             P(("grp", "ap", "sq"), "tp"),

time: 225 us -> 165 us (0.73)
  waiting for transfers between devices: 37.2 us -> 0 us
  between operations: 14.2 us -> 0.71 us
  matrix products: 7.03 us -> 0 us
  starting transfers between devices: 4.84 us -> 0 us
  local copies, waits for them, and re-layouts: 7.94 us -> 10.3 us
    psum x1 -> x0, waiting for transfers between devices: 37.1 us -> none  [on_device(): rank_act = lax.psum(rank_part, 'tp')]
    dot_general x2 -> x0, matrix products: 7.03 us -> none  [the longest x1 5.61 us: on_device(): jnp.einsum('qsk,qkn->qsn', rank_act, up.astype(jnp.float32), precision=la...]
    all_to_all x1 -> x0, starting transfers between devices: 4.8 us -> none  [on_device(): moved = lax.all_to_all(picked, 'ap', 0, 0)]
  transfers between devices with their start and end apart: 2 -> 0, of which waited for: 1 -> 0; matrix products, arithmetic and copies ran while one was open for 0% -> 0% of each run, Pallas kernels for 64% -> 0%
where the time goes in v2:
time: 165 us; the launch traced here: 163 us
  Pallas kernels  145 us (88%)
  local copies, waits for them, and re-layouts  10.3 us (6%)
  blocking collectives  5.19 us (3%)
  other arithmetic  2.41 us (1%)
    pallas_call x1, Pallas kernels, line_sum(): pl.pallas_call(functools.partial(line_kernel, n, n_ap, chunks, cw, req),...  145 us
    gather x2, local copies, waits for them, and re-layouts, on_device(): store[place]  5.6 us
    unnamed x1, blocking collectives  5.19 us
    unnamed x10, local copies, waits for them, and re-layouts  3.61 us

profile of v2, /device:TPU:0, one launch (start us, length us, event | category | flops | bytes accessed | tf_op | source)
XLA Modules:
  0.0 163.3 jit_solution(10905848596839065464)
XLA Ops:
  0.0 0.0 copy-start
  0.0 1.2 dynamic-slice
  1.9 0.7 compare_select_fusion.1
  2.6 0.0 copy-done
  2.6 0.6 gather_fusion
  3.2 0.2 dynamic-update-slice
  3.4 5.2 %all-reduce = s32[4]{0:T(128)S(1)} all-reduce(s32[4]{0:T(128)S(1)} %dynamic-update-slice), channel_id=2, replica_groups=mesh['grp'=2,'tp'=4,'ap'=2,'sq'=2] {'ap'}, use_global_device_ids=true, to_apply=%add | all-reduce | flops 4 | bytes 32
  8.6 0.1 reshape.69
  8.7 0.1 broadcast_in_dim.29
  8.8 0.1 broadcast_in_dim.30
  8.9 0.1 reshape.68
  9.0 0.1 reshape.38
  9.1 2.8 %gather_fusion.2 = bf16[4,64,2048]{2,1,0:T(8,128)(2,1)S(1)} fusion(bf16[16,64,2048]{2,1,0:T(8,128)(2,1)} %param.10, s32[1024]{0:T(1024)S(1)} %pad_clamp_fusion), kind=kCustom, calls=%fused_computation.2 | custom fusion | bytes 2097168 | tf_op jit(solution)/shard_map/gather | solution.py:344
  11.9 2.8 %gather_fusion.1 = bf16[4,64,2048]{2,1,0:T(8,128)(2,1)S(1)} fusion(bf16[16,64,2048]{2,1,0:T(8,128)(2,1)} %param.9, s32[1024]{0:T(1024)S(1)} %pad_clamp_fusion), kind=kCustom, calls=%fused_computation.1 | custom fusion | bytes 2097168 | tf_op jit(solution)/shard_map/gather | solution.py:344
  14.7 0.2 broadcast_select_fusion.1
  14.9 0.0 copy-start.1
  14.9 0.0 copy-start.2
  14.9 1.5 pad_maximum_fusion.picked_ref
  16.4 0.8 copy-done.1
  17.2 0.0 copy-done.2
  17.2 144.8 %shard_map.73 = bf16[512,2048]{1,0:T(8,128)(2,1)S(1)} custom-call(bf16[512,2048]{1,0:T(8,128)(2,1)S(1)} %copy-done.1, bf16[2048,8192]{1,0:T(8,128)(2,1)} %w_ref.1, bf16[2,2,128,2048]{3,2,1,0:T(8,128)(2,1)} %pad_maximum_fusion.picked_ref, s32[2]{0:T(128)S(1)} %copy-done.2), custom_call_target="tpu_custom_call" | custom-call | flops 17179869184 | bytes 33554432 | tf_op jit(solution)/shard_map/pallas_call | solution.py:290
  162.0 1.3 copy.10
  (6 shorter events, 0.0 us)
Async XLA Ops:
  0.0 2.6 %copy-start = (s32[32]{0:T(128)S(1)}, s32[32]{0:T(128)}, u32[]{:S(2)}) copy-start(s32[32]{0:T(128)} %param.12) | copy-start | bytes 388
  14.9 2.4 %copy-start.1 = (bf16[512,2048]{1,0:T(8,128)(2,1)S(1)}, bf16[512,2048]{1,0:T(8,128)(2,1)}, u32[]{:S(2)}) copy-start(bf16[512,2048]{1,0:T(8,128)(2,1)} %x_ref.1) | copy-start | bytes 6291460
  14.9 2.3 %copy-start.2 = (s32[2]{0:T(128)S(1)}, s32[2]{0:T(128)}, u32[]{:S(2)}) copy-start(s32[2]{0:T(128)} %length_ref.1) | copy-start | bytes 28

commit v3 on v2

--- a/solution.py
+++ b/solution.py
@@ -10,29 +10,19 @@
 MESH = pl.DeviceIdType.MESH
 SLOTS = 3
 TOP = 32500.0
-STEPS = 64.0
-
-
-def decode(ref, rows):
-    power = ref[rows : rows + 16, :][0:1, :].astype(jnp.float32)
-    scale = jnp.exp2(power * (1.0 / STEPS)) * (1.0 / TOP)
-    return ref[0:rows, :].astype(jnp.float32) * scale
-
-
-def encode(ref, value, rows):
+
+
+def encode(ref, scale_ref, value):
     top = jnp.maximum(jnp.max(jnp.abs(value), axis=0, keepdims=True), 1e-30)
-    power = jnp.ceil(jnp.log2(top) * STEPS)
-    factor = jnp.exp2(power * (-1.0 / STEPS)) * TOP
-    ref[0:rows, :] = jnp.round(value * factor).astype(jnp.int32).astype(jnp.int16)
-    ref[rows : rows + 16, :] = (
-        jnp.broadcast_to(power, (16, power.shape[1])).astype(jnp.int32).astype(jnp.int16)
-    )
+    scale_ref[...] = top * (1.0 / TOP)
+    ref[...] = jnp.round(value * (TOP / top)).astype(jnp.int32).astype(jnp.int16)
 
 
 def line_kernel(
-    n, n_ap, chunks, cw, req, x_ref, w_ref, picked_ref, length_ref, o_ref, inbox, outbox, wbuf, own_w, acc,
-    factors, up, rank_own, rank_in, rank_out, parts, recv_sem, send_sem, w_sem, own_sem,
-    factor_recv, factor_send, rank_recv, rank_send, local_sem,
+    n, n_ap, chunks, cw, req, x_ref, w_ref, shrink_ref, expand_ref, adapter_ref, slot_ref, length_ref,
+    o_ref, inbox, outbox, in_scale, out_scale, wbuf, own_w, acc,
+    stores, ids_in, ids_out, picked, factors, up, rank_own, rank_in, rank_out, parts, recv_sem, send_sem, w_sem, own_sem,
+    scale_recv, scale_send, ids_recv, ids_send, factor_recv, factor_send, rank_recv, rank_send, store_sem,
 ):
     i = lax.axis_index("tp")
     me = lax.axis_index("ap")
@@ -42,18 +32,34 @@
     bw = chunks * cw
     items = chunks * (n - 1)
     middle = items // 3
+    early = min(2, middle)
     count_right = chunks * (n - 1 - i)
     count_left = chunks * i
 
+    def ids_copy(hop):
+        return pltpu.make_async_remote_copy(
+            src_ref=ids_out,
+            dst_ref=ids_in.at[hop],
+            send_sem=ids_send.at[hop],
+            recv_sem=ids_recv.at[hop],
+            device_id={"ap": (me + hop) % n_ap},
+            device_id_type=MESH,
+        )
+
     def factor_copy(hop):
         return pltpu.make_async_remote_copy(
-            src_ref=picked_ref.at[(me + hop) % n_ap],
-            dst_ref=factors.at[me],
+            src_ref=picked.at[hop],
+            dst_ref=factors.at[hop],
             send_sem=factor_send.at[hop],
             recv_sem=factor_recv.at[hop],
-            device_id={"ap": (me + hop) % n_ap},
+            device_id={"ap": (me + n_ap - hop) % n_ap},
             device_id_type=MESH,
         )
+
+    store_copies = [
+        pltpu.make_async_copy(ref, stores.at[which], store_sem.at[which])
+        for which, ref in enumerate((shrink_ref, expand_ref))
+    ]
 
     def rank_copy(way):
         return pltpu.make_async_remote_copy(
@@ -65,7 +71,8 @@
             device_id_type=MESH,
         )
 
-    own_factors = pltpu.make_async_copy(picked_ref.at[me], factors.at[me], local_sem)
+    held = stores.shape[1]
+    own_slots = [slot_ref[adapter_ref[q]] for q in range(req)]
 
     def weight_copy(way, k):
         block = jnp.where(way == 0, n - 1 - k // chunks, k // chunks)
@@ -91,6 +98,17 @@
             device_id_type=MESH,
         )
 
+    def scale_copy(way, k):
+        target = jnp.clip(i + 1 - 2 * way, 0, n - 1)
+        return pltpu.make_async_remote_copy(
+            src_ref=out_scale.at[way, k % SLOTS],
+            dst_ref=in_scale.at[way, k],
+            send_sem=scale_send.at[way, k % SLOTS],
+            recv_sem=scale_recv.at[way, k],
+            device_id={"tp": target},
+            device_id_type=MESH,
+        )
+
     def count_of(way):
         return jnp.where(way == 0, count_right, count_left)
 
@@ -103,7 +121,13 @@
         weight_copy(1, 0).start()
 
     own_copy(0).start()
-    own_factors.start()
+    for copy in store_copies:
+        copy.start()
+    line = lax.broadcasted_iota(jnp.int32, ids_out.shape, 0)
+    listed = jnp.zeros(ids_out.shape, jnp.int32)
+    for q in range(req):
+        listed = jnp.where(line == q, own_slots[q], listed)
+    ids_out[...] = listed
 
     barrier = pltpu.get_barrier_semaphore()
 
@@ -125,7 +149,7 @@
     )
 
     for hop in range(1, n_ap):
-        factor_copy(hop).start()
+        ids_copy(hop).start()
 
     late = jnp.where(i >= n // 2, 1, 0)
 
@@ -134,9 +158,31 @@
         way = (t + late) % 2
         count = count_of(way)
 
+        @pl.when(t == 2 * early)
+        def _():
+            for copy in store_copies:
+                copy.wait()
+            for hop in range(n_ap):
+                if hop > 0:
+                    ids_copy(hop).wait_recv()
+                for q in range(req):
+                    slot = own_slots[q] if hop == 0 else jnp.max(ids_in[hop, q : q + 1, :])
+                    place = slot - me * held
+                    here = (place >= 0) & (place < held)
+                    place = jnp.clip(place, 0, held - 1)
+                    for which in range(2):
+                        value = stores[which, place]
+                        value = jnp.where(here, value, jnp.zeros_like(value))
+                        span = slice(q * rank, (q + 1) * rank)
+                        if hop == 0:
+                            factors[0, which, span, :] = value
+                        else:
+                            picked[hop, which, span, :] = value
+                if hop > 0:
+                    factor_copy(hop).start()
+
         @pl.when(t == 2 * middle)
         def _():
-            own_factors.wait()
             for hop in range(1, n_ap):
                 factor_copy(hop).wait_recv()
             down = factors[0, 0]
@@ -180,13 +226,16 @@
             @pl.when(jnp.where(way == 0, i, n - 1 - i) > 0)
             def _():
                 item_copy(way, k).wait_recv()
-                acc[...] += decode(inbox.at[way, k], rows)
+                scale_copy(way, k).wait_recv()
+                acc[...] += inbox[way, k].astype(jnp.float32) * in_scale[way, k]
 
             @pl.when(k >= SLOTS)
             def _():
                 item_copy(way, k).wait_send()
-
-            encode(outbox.at[way, k % SLOTS], acc[...], rows)
+                scale_copy(way, k).wait_send()
+
+            encode(outbox.at[way, k % SLOTS], out_scale.at[way, k % SLOTS], acc[...])
+            scale_copy(way, k).start()
             item_copy(way, k).start()
 
         return carry
@@ -238,13 +287,15 @@
         def _():
             k = count_right + c
             item_copy(0, k).wait_recv()
-            acc[...] += decode(inbox.at[0, k], rows)
+            scale_copy(0, k).wait_recv()
+            acc[...] += inbox[0, k].astype(jnp.float32) * in_scale[0, k]
 
         @pl.when(i < n - 1)
         def _():
             k = count_left + c
             item_copy(1, k).wait_recv()
-            acc[...] += decode(inbox.at[1, k], rows)
+            scale_copy(1, k).wait_recv()
+            acc[...] += inbox[1, k].astype(jnp.float32) * in_scale[1, k]
 
         for q in range(req):
             span = slice(q * slot_rows, (q + 1) * slot_rows)
@@ -263,12 +314,14 @@
         @pl.when(k >= 0)
         def _():
             item_copy(way, k).wait_send()
+            scale_copy(way, k).wait_send()
 
         return carry
 
     lax.fori_loop(0, 2 * SLOTS, drain, 0)
 
     for hop in range(1, n_ap):
+        ids_copy(hop).wait_send()
         factor_copy(hop).wait_send()
     for way in range(2):
 
@@ -277,11 +330,15 @@
             rank_copy(way).wait_send()
 
 
-def line_sum(n, n_ap, heads_out, base_weight, picked, prompt_length):
+def line_sum(
+    n, n_ap, heads_out, base_weight, shrink_store, expand_store, request_adapter, adapter_slot, prompt_length
+):
     rows, depth = heads_out.shape
     width = base_weight.shape[1]
     req = prompt_length.shape[0]
-    lanes = picked.shape[2]
+    held, rank, part = shrink_store.shape
+    lanes = req * rank
+    ids_rows = -(-req // 8) * 8
     bw = width // n
     cw = min(256, bw)
     chunks = bw // cw
@@ -294,16 +351,25 @@
             pl.BlockSpec(memory_space=pltpu.VMEM),
             pl.BlockSpec(memory_space=pl.ANY),
             pl.BlockSpec(memory_space=pl.ANY),
+            pl.BlockSpec(memory_space=pl.ANY),
+            pl.BlockSpec(memory_space=pltpu.SMEM),
+            pl.BlockSpec(memory_space=pltpu.SMEM),
             pl.BlockSpec(memory_space=pltpu.SMEM),
         ],
         out_specs=pl.BlockSpec(memory_space=pltpu.VMEM),
         scratch_shapes=[
-            pltpu.VMEM((2, items, rows + 16, cw), jnp.int16),
-            pltpu.VMEM((2, SLOTS, rows + 16, cw), jnp.int16),
+            pltpu.VMEM((2, items, rows, cw), jnp.int16),
+            pltpu.VMEM((2, SLOTS, rows, cw), jnp.int16),
+            pltpu.VMEM((2, items, 1, cw), jnp.float32),
+            pltpu.VMEM((2, SLOTS, 1, cw), jnp.float32),
             pltpu.VMEM((2, 2, depth, cw), jnp.bfloat16),
             pltpu.VMEM((2, depth, cw), jnp.bfloat16),
             pltpu.VMEM((rows, cw), jnp.float32),
-            pltpu.VMEM(picked.shape, jnp.bfloat16),
+            pltpu.VMEM((2, held, rank, part), jnp.bfloat16),
+            pltpu.VMEM((n_ap, ids_rows, 128), jnp.int32),
+            pltpu.VMEM((ids_rows, 128), jnp.int32),
+            pltpu.VMEM((n_ap, 2, lanes, part), jnp.bfloat16),
+            pltpu.VMEM((n_ap, 2, lanes, part), jnp.bfloat16),
             pltpu.VMEM((lanes, depth), jnp.bfloat16),
             pltpu.VMEM((slot_rows, lanes), jnp.float32),
             pltpu.VMEM((2, slot_rows, lanes), jnp.float32),
@@ -313,11 +379,15 @@
             pltpu.SemaphoreType.DMA((2, SLOTS)),
             pltpu.SemaphoreType.DMA((2, 2)),
             pltpu.SemaphoreType.DMA((2,)),
+            pltpu.SemaphoreType.DMA((2, items)),
+            pltpu.SemaphoreType.DMA((2, SLOTS)),
+            pltpu.SemaphoreType.DMA((n_ap,)),
+            pltpu.SemaphoreType.DMA((n_ap,)),
             pltpu.SemaphoreType.DMA((n_ap,)),
             pltpu.SemaphoreType.DMA((n_ap,)),
             pltpu.SemaphoreType.DMA((2,)),
             pltpu.SemaphoreType.DMA((2,)),
-            pltpu.SemaphoreType.DMA,
+            pltpu.SemaphoreType.DMA((2,)),
         ],
         compiler_params=pltpu.CompilerParams(
             collective_id=0, has_side_effects=True, vmem_limit_bytes=48 * 1024 * 1024
@@ -327,29 +397,12 @@
             bytes_accessed=2 * depth * width,
             transcendentals=0,
         ),
-    )(heads_out, base_weight, picked, prompt_length)
-
-
-def on_device(
-    n, n_ap, heads_out, base_weight, shrink_store, expand_store, request_adapter, adapter_slot, prompt_length
-):
-    held, rank, part = shrink_store.shape
-    req = request_adapter.shape[0]
-    slot_ids = adapter_slot[request_adapter]
-    wanted = lax.all_gather(slot_ids, "ap") - lax.axis_index("ap") * held
-    here = ((wanted >= 0) & (wanted < held))[:, :, None, None]
-    place = jnp.clip(wanted, 0, held - 1)
-    zero = jnp.zeros((), shrink_store.dtype)
-    picked = jnp.stack(
-        [jnp.where(here, store[place], zero) for store in (shrink_store, expand_store)], axis=1
-    )
-    picked = picked.reshape(n_ap, 2, req * rank, part)
-    return line_sum(n, n_ap, heads_out, base_weight, picked, prompt_length)
+    )(heads_out, base_weight, shrink_store, expand_store, request_adapter, adapter_slot, prompt_length)
 
 
 def solution(mesh):
     return jax.shard_map(
-        functools.partial(on_device, mesh.shape["tp"], mesh.shape["ap"]),
+        functools.partial(line_sum, mesh.shape["tp"], mesh.shape["ap"]),
         mesh=mesh,
         in_specs=(
             P(("grp", "ap", "sq"), "tp"),

time: 165 us -> 151 us (0.915)
  local copies, waits for them, and re-layouts: 10.3 us -> 4.88 us
  blocking collectives: 5.19 us -> 0 us
  other arithmetic: 2.41 us -> 0 us
    gather x3 -> x0, local copies, waits for them, and re-layouts: 6.24 us -> none  [the longest x2 5.6 us: on_device(): store[place]]
    unnamed x1 -> x0, blocking collectives: 5.19 us -> none
    unnamed x10 -> x9, local copies, waits for them, and re-layouts: 3.61 us -> 4.88 us
where the time goes in v3:
time: 151 us; the launch traced here: 149 us
  Pallas kernels  144 us (95%)
  local copies, waits for them, and re-layouts  4.88 us (3%)
    pallas_call x1, Pallas kernels, line_sum(): pl.pallas_call(functools.partial(line_kernel, n, n_ap, chunks, cw, req),...  144 us
    unnamed x9, local copies, waits for them, and re-layouts  4.88 us

profile of v3, /device:TPU:0, one launch (start us, length us, event | category | flops | bytes accessed | tf_op | source)
XLA Modules:
  0.0 148.9 jit_solution(10844663916415053952)
XLA Ops:
  0.0 0.0 copy-start
  0.0 1.6 %copy-done = bf16[512,2048]{1,0:T(8,128)(2,1)S(1)} copy-done((bf16[512,2048]{1,0:T(8,128)(2,1)S(1)}, bf16[512,2048]{1,0:T(8,128)(2,1)}, u32[]{:S(2)}) %copy-start) | copy-done | bytes 2097176
  1.6 0.0 copy-start.1
  1.6 0.7 copy-done.1
  2.2 0.0 copy-start.2
  2.2 0.7 copy-done.2
  2.9 0.0 copy-start.3
  2.9 0.7 copy-done.3
  3.6 144.0 %shard_map.73 = bf16[512,2048]{1,0:T(8,128)(2,1)S(1)} custom-call(bf16[512,2048]{1,0:T(8,128)(2,1)S(1)} %copy-done, bf16[2048,8192]{1,0:T(8,128)(2,1)} %w_ref.1, bf16[16,64,2048]{2,1,0:T(8,128)(2,1)} %shrink_ref.1, bf16[16,64,2048]{2,1,0:T(8,128)(2,1)} %expand_ref.1, s32[2]{0:T(128)S(1)} %copy-done.1, s32[32]{0:T(128)S(1)} %copy-done.2, s32[2]{0:T(128)S(1)} %copy-done.3), custom_call_target="tpu_custom_call" | custom-call | flops 17179869184 | bytes 33554432 | tf_op jit(solution)/shard_map/pallas_call | solution.py:347
  147.6 1.3 copy.9
Async XLA Ops:
  0.0 1.6 %copy-start = (bf16[512,2048]{1,0:T(8,128)(2,1)S(1)}, bf16[512,2048]{1,0:T(8,128)(2,1)}, u32[]{:S(2)}) copy-start(bf16[512,2048]{1,0:T(8,128)(2,1)} %x_ref.1) | copy-start | bytes 6291460
  1.6 0.7 copy-start.1
  2.2 0.7 copy-start.2
  2.9 0.7 copy-start.3

commit v4 on v3

--- a/solution.py
+++ b/solution.py
@@ -19,10 +19,11 @@
 
 
 def line_kernel(
-    n, n_ap, chunks, cw, req, x_ref, w_ref, shrink_ref, expand_ref, adapter_ref, slot_ref, length_ref,
-    o_ref, inbox, outbox, in_scale, out_scale, wbuf, own_w, acc,
+    n, n_ap, chunks, cw, req, x_hbm, w_ref, shrink_ref, expand_ref, adapter_ref, slot_ref, length_ref,
+    o_hbm, x_ref, o_ref, inbox, outbox, in_scale, out_scale, wbuf, own_w, acc,
     stores, ids_in, ids_out, picked, factors, up, rank_own, rank_in, rank_out, parts, recv_sem, send_sem, w_sem, own_sem,
     scale_recv, scale_send, ids_recv, ids_send, factor_recv, factor_send, rank_recv, rank_send, store_sem,
+    x_sem, o_sem,
 ):
     i = lax.axis_index("tp")
     me = lax.axis_index("ap")
@@ -31,8 +32,8 @@
     rank = lanes // req
     bw = chunks * cw
     items = chunks * (n - 1)
-    middle = items // 3
-    early = min(2, middle)
+    middle = max(1, items // 3)
+    early = max(1, min(2, middle))
     count_right = chunks * (n - 1 - i)
     count_left = chunks * i
 
@@ -112,6 +113,9 @@
     def count_of(way):
         return jnp.where(way == 0, count_right, count_left)
 
+    x_copy = pltpu.make_async_copy(x_hbm, x_ref, x_sem)
+    x_copy.start()
+
     @pl.when(count_right > 0)
     def _():
         weight_copy(0, 0).start()
@@ -120,9 +124,6 @@
     def _():
         weight_copy(1, 0).start()
 
-    own_copy(0).start()
-    for copy in store_copies:
-        copy.start()
     line = lax.broadcasted_iota(jnp.int32, ids_out.shape, 0)
     listed = jnp.zeros(ids_out.shape, jnp.int32)
     for q in range(req):
@@ -151,12 +152,20 @@
     for hop in range(1, n_ap):
         ids_copy(hop).start()
 
+    x_copy.wait()
+
     late = jnp.where(i >= n // 2, 1, 0)
 
     def step(t, carry):
         k = t // 2
         way = (t + late) % 2
         count = count_of(way)
+
+        @pl.when(t == 1)
+        def _():
+            own_copy(0).start()
+            for copy in store_copies:
+                copy.start()
 
         @pl.when(t == 2 * early)
         def _():
@@ -268,6 +277,10 @@
 
     position = lax.broadcasted_iota(jnp.int32, (slot_rows, cw), 0)
 
+    def out_copy(c):
+        here = pl.ds(pl.multiple_of(c * cw, cw), cw)
+        return pltpu.make_async_copy(o_ref.at[:, here], o_hbm.at[:, here], o_sem.at[c])
+
     def finish(c, carry):
         own_copy(c).wait()
 
@@ -302,6 +315,7 @@
             o_ref[span, here] = jnp.where(
                 position < length_ref[q], acc[span, :], 0.0
             ).astype(jnp.bfloat16)
+        out_copy(c).start()
         return carry
 
     lax.fori_loop(0, chunks, finish, 0)
@@ -319,6 +333,12 @@
         return carry
 
     lax.fori_loop(0, 2 * SLOTS, drain, 0)
+
+    def leave(c, carry):
+        out_copy(c).wait()
+        return carry
+
+    lax.fori_loop(0, chunks, leave, 0)
 
     for hop in range(1, n_ap):
         ids_copy(hop).wait_send()
@@ -348,7 +368,7 @@
         functools.partial(line_kernel, n, n_ap, chunks, cw, req),
         out_shape=jax.ShapeDtypeStruct((rows, bw), jnp.bfloat16),
         in_specs=[
-            pl.BlockSpec(memory_space=pltpu.VMEM),
+            pl.BlockSpec(memory_space=pl.ANY),
             pl.BlockSpec(memory_space=pl.ANY),
             pl.BlockSpec(memory_space=pl.ANY),
             pl.BlockSpec(memory_space=pl.ANY),
@@ -356,8 +376,10 @@
             pl.BlockSpec(memory_space=pltpu.SMEM),
             pl.BlockSpec(memory_space=pltpu.SMEM),
         ],
-        out_specs=pl.BlockSpec(memory_space=pltpu.VMEM),
+        out_specs=pl.BlockSpec(memory_space=pl.ANY),
         scratch_shapes=[
+            pltpu.VMEM((rows, depth), jnp.bfloat16),
+            pltpu.VMEM((rows, bw), jnp.bfloat16),
             pltpu.VMEM((2, items, rows, cw), jnp.int16),
             pltpu.VMEM((2, SLOTS, rows, cw), jnp.int16),
             pltpu.VMEM((2, items, 1, cw), jnp.float32),
@@ -388,9 +410,11 @@
             pltpu.SemaphoreType.DMA((2,)),
             pltpu.SemaphoreType.DMA((2,)),
             pltpu.SemaphoreType.DMA((2,)),
+            pltpu.SemaphoreType.DMA,
+            pltpu.SemaphoreType.DMA((chunks,)),
         ],
         compiler_params=pltpu.CompilerParams(
-            collective_id=0, has_side_effects=True, vmem_limit_bytes=48 * 1024 * 1024
+            collective_id=0, has_side_effects=True, vmem_limit_bytes=62 * 1024 * 1024
         ),
         cost_estimate=pl.CostEstimate(
             flops=2 * rows * depth * width,

time: 151 us -> 149 us (0.987)
  local copies, waits for them, and re-layouts: 4.88 us -> 3.16 us
    unnamed x9 -> x1, local copies, waits for them, and re-layouts: 4.88 us -> 3.16 us
where the time goes in v4:
time: 149 us; the launch traced here: 147 us
  Pallas kernels  144 us (97%)
  local copies, waits for them, and re-layouts  3.16 us (2%)
    pallas_call x1, Pallas kernels, line_sum(): pl.pallas_call(functools.partial(line_kernel, n, n_ap, chunks, cw, req),...  144 us
    unnamed x1, local copies, waits for them, and re-layouts  3.16 us

profile of v4, /device:TPU:0, one launch (start us, length us, event | category | flops | bytes accessed | tf_op | source)
XLA Modules:
  0.0 147.1 jit_solution(2397530176974874163)
XLA Ops:
  0.0 143.9 %shard_map.73 = bf16[512,2048]{1,0:T(8,128)(2,1)} custom-call(bf16[512,2048]{1,0:T(8,128)(2,1)} %x_hbm.1, bf16[2048,8192]{1,0:T(8,128)(2,1)} %w_ref.1, bf16[16,64,2048]{2,1,0:T(8,128)(2,1)} %shrink_ref.1, bf16[16,64,2048]{2,1,0:T(8,128)(2,1)} %expand_ref.1, s32[2]{0:T(128)} %adapter_ref.1, s32[32]{0:T(128)} %slot_ref.1, s32[2]{0:T(128)} %length_ref.1), custom_call_target="tpu_custom_call" | custom-call | flops 17179869184 | bytes 33554432 | tf_op jit(solution)/shard_map/pallas_call | solution.py:367
  144.0 3.2 %copy.9 = bf16[512,2048]{1,0:T(8,128)(2,1)} copy(bf16[512,2048]{1,0:T(8,128)(2,1)} %shard_map.73) | data formatting | bytes 4194304
